TPU v7x, 32 devices: a whole 2x2x4 slice. The times are simulated.
32 devices in a mesh: strip: 4 (over x, core), blk: 8 (over z, y).
Axes of the slice: x: 2, y: 2, z: 4, core: 2. Of those that a mesh axis runs over, the one named last changes fastest.
Arguments:
- objects: float32 [2, 2, 512, 1024], P(None, None, 'strip', 'blk'), may hold values from 0.5 to 1
- probe_init: float32 [2, 64, 256], replicated, may hold values from -1 to 1
- scan_rows: int32 [64], P(('strip', 'blk')), may hold values from 0 to 64
- scan_cols: int32 [64], P(('strip', 'blk')), may hold values from 0 to 64
- amplitudes: float32 [64, 4096], P(('strip', 'blk')), may hold values from 0.5 to 2.5
- counts: int32 [32], P(('strip', 'blk')), may hold values from 1 to 2, 48 in all
- offsets: int32 [4], replicated, may hold values from 0 to 127
Outputs:
- refined_object: float32 [2, 2, 512, 1024], P(None, None, 'strip', 'blk')
- probe_step: float32 [2, 64, 256], P(None, None, 'blk')
Inputs may be any that keep to these rules, and one draw needn't show every extreme that they name: `counts`: A device's slots from its count on are unused. `offsets`: the last entry is unused.
All inputs are finite; a program needn't handle non-finite values.
Results may differ from a plain program's by a relative error of at most 0.0001.
Values sent between devices are 32-bit elements; how exact they have to be, the bound alone decides.
A program may use at most 64 MiB of HBM per device.

v0:
```python
import functools

import jax
import jax.numpy as jnp
import ml_dtypes
import numpy as np
from jax import lax
from jax.experimental import pallas as pl
from jax.experimental.pallas import tpu as pltpu
from jax.sharding import PartitionSpec as P

ROUNDS = 2
BORDER = 32
object_rate = 0.3
probe_rate = 0.5
modulus_floor = 0.25
fresnel_phase = 0.15
power_epsilon = 1e-06
MESH = pl.DeviceIdType.MESH


def two_parts(table):
    high = table.astype(ml_dtypes.bfloat16)
    low = (table - high.astype(np.float64)).astype(ml_dtypes.bfloat16)
    return [high, low]


def tables_of(window, modes):
    position = np.arange(window)
    angle = (position[:, None] * position[None, :] % window) * (2 * np.pi / window)
    dft = (np.cos(angle) - 1j * np.sin(angle)) / np.sqrt(window)
    frequency = np.where(position < window // 2, position, position - window)
    phase = np.exp(1j * fresnel_phase * frequency.astype(np.float64) ** 2 / window)
    fresnel = np.conj(dft) @ (phase[:, None] * dft)
    left, right = [], []
    for matrix in (dft, np.conj(dft), fresnel, np.conj(fresnel)):
        left += two_parts(np.block([[matrix.real, -matrix.imag], [matrix.imag, matrix.real]]))
    for matrix in (dft, fresnel):
        for part in (matrix.real, matrix.imag):
            right += two_parts(np.kron(np.eye(modes), part))
    return np.stack(left), np.stack(right)


def halves(value):
    high = value.astype(jnp.bfloat16)
    return high, (value - high.astype(jnp.float32)).astype(jnp.bfloat16)


def product(left, right):
    return jnp.dot(left, right, preferred_element_type=jnp.float32)


def kernel(
    n_strip, n_blk,
    rows_ref, cols_ref, counts_ref, offsets_ref,
    objects_ref, probe_ref, amps_ref, left_ref, right_ref,
    out_ref, step_ref,
    tile, spread, probe_out, probe_in,
    shares, arrived, partial, strips, rims,
    ring_sems, share_send, share_recv, strip_send, strip_recv, rim_send, rim_recv,
):
    s, b = lax.axis_index("strip"), lax.axis_index("blk")
    window, width = probe_ref.shape[1], probe_ref.shape[2]
    modes = width // window
    slots = amps_ref.shape[0]
    size = objects_ref.shape[2]
    share = shares.shape[1]
    groups = 128 // share

    def blk_step(k):
        return lax.rem(b + k + n_blk, n_blk)

    def strip_step(k):
        return lax.rem(s + k + n_strip, n_strip)

    rims[...] = jnp.zeros_like(rims)
    barrier = pltpu.get_barrier_semaphore()
    partners = [(s, blk_step(k)) for k in range(1, n_blk)]
    partners += [(strip_step(k), b) for k in range(1, n_strip)]
    partners += [(strip_step(k), blk_step(k)) for k in (-1, 1)]
    for partner in partners:
        pl.semaphore_signal(barrier, inc=1, device_id=partner, device_id_type=MESH)

    def transform(pairs, left_index, right_index, sign):
        left_high, left_low = left_ref[left_index], left_ref[left_index + 1]
        middles = []
        for re, im in pairs:
            high, low = halves(jnp.concatenate([re, im], axis=0))
            middles.append(product(left_high, high) + product(left_high, low) + product(left_low, high))
        high, low = halves(jnp.concatenate(middles, axis=0))
        sums = []
        for index in (right_index, right_index + 2):
            table_high, table_low = right_ref[index], right_ref[index + 1]
            sums.append(product(high, table_high) + product(high, table_low) + product(low, table_high))
        by_re, by_im = sums
        results = []
        for j in range(len(pairs)):
            re_rows = slice(2 * j * window, (2 * j + 1) * window)
            im_rows = slice((2 * j + 1) * window, (2 * j + 2) * window)
            if sign > 0:
                results.append((by_re[re_rows] - by_im[im_rows], by_im[re_rows] + by_re[im_rows]))
            else:
                results.append((by_re[re_rows] + by_im[im_rows], by_re[im_rows] - by_im[re_rows]))
        return results

    def times(x, y):
        return x[0] * y[0] - x[1] * y[1], x[0] * y[1] + x[1] * y[0]

    def conj_times(x, y):
        return x[0] * y[0] + x[1] * y[1], x[0] * y[1] - x[1] * y[0]

    lane = lax.broadcasted_iota(jnp.int32, (window, 128), 1)

    def over_modes(value):
        total = value[:, :128]
        for start in range(128, width, 128):
            total = total + value[:, start : start + 128]
        return total + pltpu.roll(total, window, 1)

    def widened(value):
        return jnp.concatenate([value] * (width // 128), axis=1)

    def window_of(source, part, layer, j):
        rows = source[part, layer, pl.ds(rows_ref[j], window), :]
        rows = pltpu.roll(rows, lax.rem(size - cols_ref[j], size), 1)
        return widened(jnp.where(lane < window, rows, pltpu.roll(rows, window, 1)))

    def total_of(value):
        return jnp.sum(jnp.sum(value, axis=0, keepdims=True), axis=1, keepdims=True)

    spread[...] = jnp.zeros_like(spread)

    def placed(buffer, value, j):
        spread[buffer, pl.ds(size - window, window), :] = jnp.where(lane < window, value, 0.0)
        rows = spread[buffer, pl.ds(size - window - rows_ref[j], size), :]
        return pltpu.roll(rows, cols_ref[j], 1)

    rim_rows = (pl.ds(0, BORDER), pl.ds(size - BORDER, BORDER))
    rim_plan = (
        (0, -1, 0, s > 0, s < n_strip - 1),
        (0, -1, -1, (s > 0) & (b > 0), (s < n_strip - 1) & (b < n_blk - 1)),
        (1, 1, 0, s < n_strip - 1, s > 0),
        (1, 1, 1, (s < n_strip - 1) & (b < n_blk - 1), (s > 0) & (b > 0)),
    )

    def rim_copy(layer, kind):
        edge, ds, db, _, _ = rim_plan[kind]
        return pltpu.make_async_remote_copy(
            src_ref=tile.at[:, layer, rim_rows[edge], :],
            dst_ref=rims.at[kind, layer],
            send_sem=rim_send.at[kind, layer],
            recv_sem=rim_recv.at[kind, layer],
            device_id=(strip_step(ds), blk_step(db)),
            device_id_type=MESH,
        )

    def send_rims(layer):
        for kind in range(4):
            @pl.when(rim_plan[kind][3])
            def _():
                rim_copy(layer, kind).start()

    ring = pltpu.make_async_remote_copy(
        src_ref=probe_out, dst_ref=probe_in,
        send_sem=ring_sems.at[0], recv_sem=ring_sems.at[1],
        device_id=(s, blk_step(1)), device_id_type=MESH,
    )

    for round_index in range(ROUNDS):
        last = round_index == ROUNDS - 1
        source = objects_ref if round_index == 0 else tile
        probe_src = probe_ref if round_index == 0 else probe_in
        powers = []
        for layer in range(2):
            squares = source[0, layer] ** 2 + source[1, layer] ** 2
            powers.append(total_of(squares) / (size * size) + power_epsilon)
        objects = [
            [(window_of(source, 0, layer, j), window_of(source, 1, layer, j)) for j in range(slots)]
            for layer in range(2)
        ]
        if round_index > 0:
            ring.wait_recv()
        probe = (probe_src[0], probe_src[1])
        probe_power = total_of(probe[0] ** 2 + probe[1] ** 2) / (window * window) + power_epsilon
        arrivals = transform([times(probe, objects[0][j]) for j in range(slots)], 4, 4, 1)
        far = transform([times(arrivals[j], objects[1][j]) for j in range(slots)], 0, 0, 1)
        changes = []
        for j in range(slots):
            weight = jnp.where(counts_ref[0] > j, 1.0, 0.0)
            modulus = jnp.sqrt(over_modes(far[j][0] ** 2 + far[j][1] ** 2))
            amps = jnp.concatenate([amps_ref[j]] * (128 // window), axis=1)
            factor = widened((amps / jnp.maximum(modulus, modulus_floor) - 1.0) * weight)
            changes.append((far[j][0] * factor, far[j][1] * factor))
        exits = transform(changes, 2, 0, -1)

        second_gain = object_rate / (probe_power * powers[0] * slots)
        for part in range(2):
            total = source[part, 1]
            for j in range(slots):
                update = over_modes(conj_times(arrivals[j], exits[j])[part]) * second_gain
                total = total + placed(2 * j + part, update, j)
            tile[part, 1] = total
        if last:
            send_rims(1)

        entries = transform([conj_times(objects[1][j], exits[j]) for j in range(slots)], 6, 4, -1)
        probe_gain = probe_rate / (powers[0] * powers[1] * slots)
        terms = [conj_times(objects[0][j], entries[j]) for j in range(slots)]
        moved = []
        for part in range(2):
            total = terms[0][part]
            for j in range(1, slots):
                total = total + terms[j][part]
            moved.append(probe[part] + probe_gain * total)
        if not last:
            for part in range(2):
                probe_out[part] = moved[part]
            if round_index == 0:
                pl.semaphore_wait(barrier, len(partners))
            ring.start()
        else:
            stacked = jnp.concatenate([moved[0] - probe_ref[0], moved[1] - probe_ref[1]], axis=0)
            group_of = lax.broadcasted_iota(jnp.int32, (share, 128), 1) // share
            for h in range(width // 128):
                for i in range(groups):
                    packed = None
                    for k in range(groups):
                        block = stacked[k * share : (k + 1) * share, h * 128 : (h + 1) * 128]
                        if k != i:
                            block = pltpu.roll(block, (k - i) % groups * share, 1)
                        packed = block if packed is None else jnp.where(group_of == k, block, packed)
                    shares[h * groups + i] = packed
            share_copies = []
            for k in range(1, n_blk):
                share_copies.append(
                    pltpu.make_async_remote_copy(
                        src_ref=shares.at[blk_step(k)], dst_ref=arrived.at[k],
                        send_sem=share_send.at[k], recv_sem=share_recv.at[k],
                        device_id=(s, blk_step(k)), device_id_type=MESH,
                    )
                )
                share_copies[-1].start()

        first_gain = object_rate / (probe_power * slots)
        for part in range(2):
            total = source[part, 0]
            for j in range(slots):
                update = over_modes(conj_times(probe, entries[j])[part]) * first_gain
                total = total + placed(2 * j + part, update, j)
            tile[part, 0] = total
        if last:
            send_rims(0)
        else:
            ring.wait_send()

    own = shares[b]
    for k in range(1, n_blk):
        share_copies[k - 1].wait_recv()
        own = own + arrived[k]
    partial[...] = own
    strip_copies = []
    for k in range(1, n_strip):
        strip_copies.append(
            pltpu.make_async_remote_copy(
                src_ref=partial, dst_ref=strips.at[k],
                send_sem=strip_send.at[k], recv_sem=strip_recv.at[k],
                device_id=(strip_step(k), b), device_id_type=MESH,
            )
        )
        strip_copies[-1].start()

    for part in range(2):
        for layer in range(2):
            out_ref[part, layer, pl.ds(BORDER, size - 2 * BORDER), :] = tile[
                part, layer, pl.ds(BORDER, size - 2 * BORDER), :
            ]
    for layer in (1, 0):
        for kind in range(4):
            @pl.when(rim_plan[kind][4])
            def _():
                rim_copy(layer, kind).wait_recv()
    column = lax.broadcasted_iota(jnp.int32, (BORDER, size), 1)
    down = offsets_ref[s]
    up = offsets_ref[jnp.maximum(s - 1, 0)]
    for layer in range(2):
        for part in range(2):
            partner = pltpu.roll(
                jnp.where(column >= down, rims[0, layer, part], rims[1, layer, part]),
                lax.rem(size - down, size), 1,
            )
            valid = (s < n_strip - 1) & ((b < n_blk - 1) | (column + down < size))
            mine = tile[part, layer, rim_rows[1], :]
            out_ref[part, layer, rim_rows[1], :] = jnp.where(valid, 0.5 * (mine + partner), mine)
            partner = pltpu.roll(
                jnp.where(column < size - up, rims[2, layer, part], rims[3, layer, part]), up, 1
            )
            valid = (s > 0) & ((b > 0) | (column >= up))
            mine = tile[part, layer, rim_rows[0], :]
            out_ref[part, layer, rim_rows[0], :] = jnp.where(valid, 0.5 * (mine + partner), mine)

    total = partial[...]
    for k in range(1, n_strip):
        strip_copies[k - 1].wait_recv()
        total = total + strips[k]
    total = total / (n_strip * n_blk)
    for k in range(groups):
        block = total if k == 0 else pltpu.roll(total, (groups - k) * share, 1)
        part, row = divmod(k * share, window)
        step_ref[part, pl.ds(row, share), :] = block[:, :share]

    for copy in share_copies + strip_copies:
        copy.wait_send()
    for layer in range(2):
        for kind in range(4):
            @pl.when(rim_plan[kind][3])
            def _():
                rim_copy(layer, kind).wait_send()


def shards(n_strip, n_blk, objects, probe_init, scan_rows, scan_cols, amplitudes, counts, offsets):
    window, width = probe_init.shape[1], probe_init.shape[2]
    slots = scan_rows.shape[0]
    size = objects.shape[2]
    share = width // n_blk
    left, right = tables_of(window, width // window)
    smem = pl.BlockSpec(memory_space=pltpu.SMEM)
    vmem = pl.BlockSpec(memory_space=pltpu.VMEM)
    dma = pltpu.SemaphoreType.DMA
    return pl.pallas_call(
        functools.partial(kernel, n_strip, n_blk),
        out_shape=(
            jax.ShapeDtypeStruct(objects.shape, jnp.float32),
            jax.ShapeDtypeStruct((2, window, share), jnp.float32),
        ),
        in_specs=[smem] * 4 + [vmem] * 5,
        out_specs=(vmem, vmem),
        scratch_shapes=[
            pltpu.VMEM(objects.shape, jnp.float32),
            pltpu.VMEM((2 * slots, 2 * size - window, size), jnp.float32),
            pltpu.VMEM(probe_init.shape, jnp.float32),
            pltpu.VMEM(probe_init.shape, jnp.float32),
            pltpu.VMEM((n_blk, share, 128), jnp.float32),
            pltpu.VMEM((n_blk, share, 128), jnp.float32),
            pltpu.VMEM((share, 128), jnp.float32),
            pltpu.VMEM((n_strip, share, 128), jnp.float32),
            pltpu.VMEM((4, 2, 2, BORDER, size), jnp.float32),
            dma((2,)),
            dma((n_blk,)), dma((n_blk,)),
            dma((n_strip,)), dma((n_strip,)),
            dma((4, 2)), dma((4, 2)),
        ],
        compiler_params=pltpu.CompilerParams(
            collective_id=0, has_side_effects=True, vmem_limit_bytes=40 * 1024 * 1024
        ),
    )(
        scan_rows, scan_cols, counts, offsets,
        objects, probe_init, amplitudes.reshape(slots, window, window),
        jnp.asarray(left), jnp.asarray(right),
    )


def solution(mesh):
    return jax.shard_map(
        functools.partial(shards, mesh.shape["strip"], mesh.shape["blk"]),
        mesh=mesh,
        in_specs=(
            P(None, None, "strip", "blk"),
            P(),
            P(("strip", "blk")),
            P(("strip", "blk")),
            P(("strip", "blk"), None),
            P(("strip", "blk")),
            P(),
        ),
        out_specs=(P(None, None, "strip", "blk"), P(None, None, "blk")),
        check_vma=False,
    )
```

profile of v0, /device:TPU:0, one launch (start us, length us, event | category | flops | bytes accessed | tf_op | source)
XLA Modules:
  0.0 30.8 jit_solution(4953183654018505539)
XLA Ops:
  1.3 0.0 copy-start.4
  1.3 0.0 copy-start.5
  1.3 0.0 copy-start.6
  1.3 0.9 %reshape.7.amps_ref = f32[2,64,64]{2,1,0:T(8,128)S(1)} reshape(f32[2,4096]{1,0:T(2,128)} %param.13) | data formatting | bytes 65536 | tf_op jit(solution)/shard_map/reshape | solution.py:357
  2.2 0.0 copy-done.4
  2.2 0.0 copy-done.5
  2.2 0.0 copy-done.6
  2.2 0.0 copy-start
  2.2 1.2 %copy-done = bf16[8,256,256]{2,1,0:T(8,128)(2,1)S(1)} copy-done((bf16[8,256,256]{2,1,0:T(8,128)(2,1)S(1)}, bf16[8,256,256]{2,1,0:T(8,128)(2,1)}, u32[]{:S(2)}) %copy-start) | copy-done | bytes 1048600
  3.4 0.0 copy-start.1
  3.4 0.9 %copy-done.1 = f32[2,2,128,128]{3,2,1,0:T(8,128)S(1)} copy-done((f32[2,2,128,128]{3,2,1,0:T(8,128)S(1)}, f32[2,2,128,128]{3,2,1,0:T(8,128)}, u32[]{:S(2)}) %copy-start.1) | copy-done | bytes 262168
  4.4 0.0 copy-start.2
  4.4 0.9 %copy-done.2 = bf16[8,128,128]{2,1,0:T(8,128)(2,1)S(1)} copy-done((bf16[8,128,128]{2,1,0:T(8,128)(2,1)S(1)}, bf16[8,128,128]{2,1,0:T(8,128)(2,1)}, u32[]{:S(2)}) %copy-start.2) | copy-done | bytes 262168
  5.3 0.0 copy-start.3
  5.3 0.9 %copy-done.3 = f32[2,64,256]{2,1,0:T(8,128)S(1)} copy-done((f32[2,64,256]{2,1,0:T(8,128)S(1)}, f32[2,64,256]{2,1,0:T(8,128)}, u32[]{:S(2)}) %copy-start.3) | copy-done | bytes 131096
  6.2 23.2 %shard_map.104 = (f32[2,2,128,128]{3,2,1,0:T(8,128)S(1)}, f32[2,64,32]{2,1,0:T(8,128)S(1)}) custom-call(s32[2]{0:T(128)S(1)} %copy-done.4, s32[2]{0:T(128)S(1)} %copy-done.5, s32[1]{0:T(128)S(6)} %copy.13.counts_ref, s32[4]{0:T(128)S(1)} %copy-done.6, f32[2,2,128,128]{3,2,1,0:T(8,128)S(1)} %copy-done.1, f32[2,64,256]{2,1,0:T(8,128)S(1)} %copy-done.3, ...), custom_call_target="tpu_custom_call" | custom-call | tf_op jit(solution)/shard_map/pallas_call | solution.py:329
  29.4 0.7 %copy.11 = f32[2,64,32]{1,2,0:T(8,128)} copy(f32[2,64,32]{2,1,0:T(8,128)S(1)} %get-tuple-element.3) | data formatting | bytes 32768 | tf_op jit(solution)/shard_map/pallas_call | solution.py:329
  30.1 0.7 %copy.14 = f32[2,2,128,128]{3,2,1,0:T(8,128)} copy(f32[2,2,128,128]{3,2,1,0:T(8,128)S(1)} %get-tuple-element.6) | data formatting | bytes 524288
Async XLA Ops:
  1.3 0.9 %copy-start.4 = (s32[2]{0:T(128)S(1)}, s32[2]{0:T(128)}, u32[]{:S(2)}) copy-start(s32[2]{0:T(128)} %rows_ref.1) | copy-start | bytes 28
  1.3 0.9 %copy-start.5 = (s32[2]{0:T(128)S(1)}, s32[2]{0:T(128)}, u32[]{:S(2)}) copy-start(s32[2]{0:T(128)} %cols_ref.1) | copy-start | bytes 28
  1.3 0.9 %copy-start.6 = (s32[4]{0:T(128)S(1)}, s32[4]{0:T(128)}, u32[]{:S(2)}) copy-start(s32[4]{0:T(128)} %offsets_ref.1) | copy-start | bytes 52
  2.2 1.2 %copy-start = (bf16[8,256,256]{2,1,0:T(8,128)(2,1)S(1)}, bf16[8,256,256]{2,1,0:T(8,128)(2,1)}, u32[]{:S(2)}) copy-start(bf16[8,256,256]{2,1,0:T(8,128)(2,1)} %constant.5.clone.right_ref) | copy-start | bytes 3145732
  3.4 0.9 %copy-start.1 = (f32[2,2,128,128]{3,2,1,0:T(8,128)S(1)}, f32[2,2,128,128]{3,2,1,0:T(8,128)}, u32[]{:S(2)}) copy-start(f32[2,2,128,128]{3,2,1,0:T(8,128)} %objects_ref.1) | copy-start | bytes 786436
  4.4 0.9 %copy-start.2 = (bf16[8,128,128]{2,1,0:T(8,128)(2,1)S(1)}, bf16[8,128,128]{2,1,0:T(8,128)(2,1)}, u32[]{:S(2)}) copy-start(bf16[8,128,128]{2,1,0:T(8,128)(2,1)} %constant.4.clone.left_ref) | copy-start | bytes 786436
  5.3 0.9 %copy-start.3 = (f32[2,64,256]{2,1,0:T(8,128)S(1)}, f32[2,64,256]{2,1,0:T(8,128)}, u32[]{:S(2)}) copy-start(f32[2,64,256]{2,1,0:T(8,128)} %probe_ref.1) | copy-start | bytes 393220
where the time goes:
time: 31.2 us; the launch traced here: 30.8 us
  Pallas kernels  23.2 us (74%)
  local copies, waits for them, and re-layouts  6.31 us (20%)
  between operations  1.33 us (4%)
    pallas_call x1, Pallas kernels, shards(): pl.pallas_call(functools.partial(kernel, n_strip, n_blk), out_shape=(jax....  23.2 us
    unnamed x15, local copies, waits for them, and re-layouts  4.74 us
    reshape x1, local copies, waits for them, and re-layouts, shards(): amplitudes.reshape(slots, window, window)  0.88 us
    pallas_call x1, local copies, waits for them, and re-layouts, shards(): pl.pallas_call(functools.partial(kernel, n_strip, n_blk), out_shape=(jax....  0.69 us

commit v1 on v0

--- a/solution.py
+++ b/solution.py
@@ -53,8 +53,9 @@
 def kernel(
     n_strip, n_blk,
     rows_ref, cols_ref, counts_ref, offsets_ref,
-    objects_ref, probe_ref, amps_ref, left_ref, right_ref,
+    objects_hbm, probe_hbm, amps_hbm, left_hbm, right_hbm,
     out_ref, step_ref,
+    objects_ref, probe_ref, amps_raw, left_ref, right_ref, amps_ref, in_sems,
     tile, spread, probe_out, probe_in,
     shares, arrived, partial, strips, rims,
     ring_sems, share_send, share_recv, strip_send, strip_recv, rim_send, rim_recv,
@@ -64,6 +65,21 @@
     modes = width // window
     slots = amps_ref.shape[0]
     size = objects_ref.shape[2]
+    both = pl.ds(0, 4), pl.ds(4, 4)
+    loads = [
+        pltpu.make_async_copy(source, target, in_sems.at[i])
+        for i, (source, target) in enumerate((
+            (objects_hbm, objects_ref),
+            (probe_hbm, probe_ref),
+            (left_hbm.at[both[1]], left_ref.at[both[1]]),
+            (right_hbm.at[both[1]], right_ref.at[both[1]]),
+            (left_hbm.at[both[0]], left_ref.at[both[0]]),
+            (right_hbm.at[both[0]], right_ref.at[both[0]]),
+            (amps_hbm, amps_raw),
+        ))
+    ]
+    for load in loads:
+        load.start()
     share = shares.shape[1]
     groups = 128 // share
 
@@ -135,6 +151,14 @@
         rows = spread[buffer, pl.ds(size - window - rows_ref[j], size), :]
         return pltpu.roll(rows, cols_ref[j], 1)
 
+    def unfold_amps():
+        first = lax.broadcasted_iota(jnp.int32, (slots, 128), 1) < window
+        for i in range(window * window // 128):
+            pair = amps_raw[:, pl.ds(128 * i, 128)]
+            turned = pltpu.roll(pair, window, 1)
+            amps_ref[:, 2 * i, :] = jnp.where(first, pair, turned)
+            amps_ref[:, 2 * i + 1, :] = jnp.where(first, turned, pair)
+
     rim_rows = (pl.ds(0, BORDER), pl.ds(size - BORDER, BORDER))
     rim_plan = (
         (0, -1, 0, s > 0, s < n_strip - 1),
@@ -170,6 +194,8 @@
         last = round_index == ROUNDS - 1
         source = objects_ref if round_index == 0 else tile
         probe_src = probe_ref if round_index == 0 else probe_in
+        if round_index == 0:
+            loads[0].wait()
         powers = []
         for layer in range(2):
             squares = source[0, layer] ** 2 + source[1, layer] ** 2
@@ -180,16 +206,22 @@
         ]
         if round_index > 0:
             ring.wait_recv()
+        else:
+            for load in loads[1:4]:
+                load.wait()
         probe = (probe_src[0], probe_src[1])
         probe_power = total_of(probe[0] ** 2 + probe[1] ** 2) / (window * window) + power_epsilon
         arrivals = transform([times(probe, objects[0][j]) for j in range(slots)], 4, 4, 1)
+        if round_index == 0:
+            for load in loads[4:]:
+                load.wait()
+            unfold_amps()
         far = transform([times(arrivals[j], objects[1][j]) for j in range(slots)], 0, 0, 1)
         changes = []
         for j in range(slots):
             weight = jnp.where(counts_ref[0] > j, 1.0, 0.0)
             modulus = jnp.sqrt(over_modes(far[j][0] ** 2 + far[j][1] ** 2))
-            amps = jnp.concatenate([amps_ref[j]] * (128 // window), axis=1)
-            factor = widened((amps / jnp.maximum(modulus, modulus_floor) - 1.0) * weight)
+            factor = widened((amps_ref[j] / jnp.maximum(modulus, modulus_floor) - 1.0) * weight)
             changes.append((far[j][0] * factor, far[j][1] * factor))
         exits = transform(changes, 2, 0, -1)
 
@@ -329,12 +361,19 @@
     return pl.pallas_call(
         functools.partial(kernel, n_strip, n_blk),
         out_shape=(
-            jax.ShapeDtypeStruct(objects.shape, jnp.float32),
-            jax.ShapeDtypeStruct((2, window, share), jnp.float32),
+            pltpu.VMEM(objects.shape, jnp.float32),
+            pltpu.VMEM((2, window, share), jnp.float32),
         ),
-        in_specs=[smem] * 4 + [vmem] * 5,
+        in_specs=[smem] * 4 + [pl.BlockSpec(memory_space=pltpu.HBM)] * 5,
         out_specs=(vmem, vmem),
         scratch_shapes=[
+            pltpu.VMEM(objects.shape, jnp.float32),
+            pltpu.VMEM(probe_init.shape, jnp.float32),
+            pltpu.VMEM(amplitudes.shape, jnp.float32),
+            pltpu.VMEM(left.shape, jnp.bfloat16),
+            pltpu.VMEM(right.shape, jnp.bfloat16),
+            pltpu.VMEM((slots, window, 128), jnp.float32),
+            dma((7,)),
             pltpu.VMEM(objects.shape, jnp.float32),
             pltpu.VMEM((2 * slots, 2 * size - window, size), jnp.float32),
             pltpu.VMEM(probe_init.shape, jnp.float32),
@@ -350,11 +389,11 @@
             dma((4, 2)), dma((4, 2)),
         ],
         compiler_params=pltpu.CompilerParams(
-            collective_id=0, has_side_effects=True, vmem_limit_bytes=40 * 1024 * 1024
+            collective_id=0, has_side_effects=True, vmem_limit_bytes=60 * 1024 * 1024
         ),
     )(
         scan_rows, scan_cols, counts, offsets,
-        objects, probe_init, amplitudes.reshape(slots, window, window),
+        objects, probe_init, amplitudes,
         jnp.asarray(left), jnp.asarray(right),
     )
 

time: 31.2 us -> 27.3 us (0.88)
  local copies, waits for them, and re-layouts: 6.31 us -> 1.39 us
  Pallas kernels: 23.2 us -> 24.4 us
    unnamed x15 -> x1, local copies, waits for them, and re-layouts: 4.74 us -> 0.71 us
    pallas_call x1, Pallas kernels: 23.2 us -> 24.4 us  [shards(): pl.pallas_call(functools.partial(kernel, n_strip, n_blk), out_shape=(pltp...]
    reshape x1 -> x0, local copies, waits for them, and re-layouts: 0.88 us -> none  [shards(): amplitudes.reshape(slots, window, window)]
where the time goes in v1:
time: 27.3 us; the launch traced here: 27.1 us
  Pallas kernels  24.4 us (89%)
  local copies, waits for them, and re-layouts  1.39 us (5%)
  between operations  1.29 us (5%)
    pallas_call x1, Pallas kernels, shards(): pl.pallas_call(functools.partial(kernel, n_strip, n_blk), out_shape=(pltp...  24.4 us
    unnamed x1, local copies, waits for them, and re-layouts  0.71 us
    pallas_call x1, local copies, waits for them, and re-layouts, shards(): pl.pallas_call(functools.partial(kernel, n_strip, n_blk), out_shape=(pltp...  0.69 us

profile of v1, /device:TPU:0, one launch (start us, length us, event | category | flops | bytes accessed | tf_op | source)
XLA Modules:
  0.0 27.1 jit_solution(16483551700107597877)
XLA Ops:
  1.3 24.4 %shard_map.104 = (f32[2,2,128,128]{3,2,1,0:T(8,128)S(1)}, f32[2,64,32]{2,1,0:T(8,128)S(1)}) custom-call(s32[2]{0:T(128)} %rows_ref.1, s32[2]{0:T(128)} %cols_ref.1, s32[1]{0:T(128)S(6)} %copy.14.counts_ref, s32[4]{0:T(128)} %offsets_ref.1, f32[2,2,128,128]{3,2,1,0:T(8,128)} %objects_hbm.1, f32[2,64,256]{2,1,0:T(8,128)} %probe_hbm.1, f32[2,4096]{1,0:T(2,128)} %amps_hbm.1, ...), custom_call_target="tpu_custom_call" | custom-call | tf_op jit(solution)/shard_map/pallas_call | solution.py:361
  25.7 0.7 %copy.13 = f32[2,2,128,128]{3,2,1,0:T(8,128)} copy(f32[2,2,128,128]{3,2,1,0:T(8,128)S(1)} %get-tuple-element.4) | data formatting | bytes 524288
  26.4 0.7 %copy.11 = f32[2,64,32]{1,2,0:T(8,128)} copy(f32[2,64,32]{2,1,0:T(8,128)S(1)} %get-tuple-element.3) | data formatting | bytes 32768 | tf_op jit(solution)/shard_map/pallas_call | solution.py:361

commit v2 on v1

--- a/solution.py
+++ b/solution.py
@@ -22,7 +22,7 @@
 def two_parts(table):
     high = table.astype(ml_dtypes.bfloat16)
     low = (table - high.astype(np.float64)).astype(ml_dtypes.bfloat16)
-    return [high, low]
+    return high, low
 
 
 def tables_of(window, modes):
@@ -32,13 +32,13 @@
     frequency = np.where(position < window // 2, position, position - window)
     phase = np.exp(1j * fresnel_phase * frequency.astype(np.float64) ** 2 / window)
     fresnel = np.conj(dft) @ (phase[:, None] * dft)
-    left, right = [], []
-    for matrix in (dft, np.conj(dft), fresnel, np.conj(fresnel)):
-        left += two_parts(np.block([[matrix.real, -matrix.imag], [matrix.imag, matrix.real]]))
-    for matrix in (dft, fresnel):
-        for part in (matrix.real, matrix.imag):
-            right += two_parts(np.kron(np.eye(modes), part))
-    return np.stack(left), np.stack(right)
+    tables = []
+    for matrix in (fresnel, dft, np.conj(dft), np.conj(fresnel)):
+        high, low = two_parts(np.block([[matrix.real, -matrix.imag], [matrix.imag, matrix.real]]))
+        pair = np.kron(np.eye(128 // window), matrix)
+        tables.append(np.block([[high, high], [low, low]]))
+        tables += two_parts(np.block([[pair.real, pair.imag], [-pair.imag, pair.real]]))
+    return np.stack(tables).astype(ml_dtypes.bfloat16)
 
 
 def halves(value):
@@ -53,9 +53,9 @@
 def kernel(
     n_strip, n_blk,
     rows_ref, cols_ref, counts_ref, offsets_ref,
-    objects_hbm, probe_hbm, amps_hbm, left_hbm, right_hbm,
+    objects_hbm, probe_hbm, amps_hbm, tables_hbm,
     out_ref, step_ref,
-    objects_ref, probe_ref, amps_raw, left_ref, right_ref, amps_ref, in_sems,
+    objects_ref, probe_ref, amps_raw, tables, amps_ref, in_sems,
     tile, spread, probe_out, probe_in,
     shares, arrived, partial, strips, rims,
     ring_sems, share_send, share_recv, strip_send, strip_recv, rim_send, rim_recv,
@@ -65,23 +65,20 @@
     modes = width // window
     slots = amps_ref.shape[0]
     size = objects_ref.shape[2]
-    both = pl.ds(0, 4), pl.ds(4, 4)
     loads = [
         pltpu.make_async_copy(source, target, in_sems.at[i])
         for i, (source, target) in enumerate((
             (objects_hbm, objects_ref),
             (probe_hbm, probe_ref),
-            (left_hbm.at[both[1]], left_ref.at[both[1]]),
-            (right_hbm.at[both[1]], right_ref.at[both[1]]),
-            (left_hbm.at[both[0]], left_ref.at[both[0]]),
-            (right_hbm.at[both[0]], right_ref.at[both[0]]),
             (amps_hbm, amps_raw),
+            *((tables_hbm.at[pl.ds(3 * i, 3)], tables.at[pl.ds(3 * i, 3)]) for i in range(4)),
         ))
     ]
     for load in loads:
         load.start()
     share = shares.shape[1]
     groups = 128 // share
+    n_pairs = width // 128
 
     def blk_step(k):
         return lax.rem(b + k + n_blk, n_blk)
@@ -97,27 +94,35 @@
     for partner in partners:
         pl.semaphore_signal(barrier, inc=1, device_id=partner, device_id_type=MESH)
 
-    def transform(pairs, left_index, right_index, sign):
-        left_high, left_low = left_ref[left_index], left_ref[left_index + 1]
+    def left_side(pairs, index):
         middles = []
         for re, im in pairs:
-            high, low = halves(jnp.concatenate([re, im], axis=0))
-            middles.append(product(left_high, high) + product(left_high, low) + product(left_low, high))
-        high, low = halves(jnp.concatenate(middles, axis=0))
-        sums = []
-        for index in (right_index, right_index + 2):
-            table_high, table_low = right_ref[index], right_ref[index + 1]
-            sums.append(product(high, table_high) + product(high, table_low) + product(low, table_high))
-        by_re, by_im = sums
+            stacked = jnp.concatenate(halves(jnp.concatenate([re, im], axis=0)), axis=0)
+            both = product(tables[3 * index], stacked)
+            total = both[: 2 * window] + both[2 * window :]
+            middles.append((total[:window], total[window:]))
+        return middles
+
+    def right_side(pairs, index):
+        rows = pairs[0][0].shape[0]
+        blocks = []
+        for re, im in pairs:
+            for start in range(0, width, 128):
+                blocks.append(jnp.concatenate([re[:, start : start + 128], im[:, start : start + 128]], axis=1))
+        high, low = halves(jnp.concatenate(blocks, axis=0))
+        count = high.shape[0]
+        both = product(jnp.concatenate([high, low], axis=0), tables[3 * index + 1])
+        total = both[:count] + both[count:] + product(high, tables[3 * index + 2])
         results = []
         for j in range(len(pairs)):
-            re_rows = slice(2 * j * window, (2 * j + 1) * window)
-            im_rows = slice((2 * j + 1) * window, (2 * j + 2) * window)
-            if sign > 0:
-                results.append((by_re[re_rows] - by_im[im_rows], by_im[re_rows] + by_re[im_rows]))
-            else:
-                results.append((by_re[re_rows] + by_im[im_rows], by_re[im_rows] - by_im[re_rows]))
+            mine = [total[(j * n_pairs + p) * rows : (j * n_pairs + p + 1) * rows] for p in range(n_pairs)]
+            results.append(tuple(
+                jnp.concatenate([x[:, part * 128 : (part + 1) * 128] for x in mine], axis=1) for part in range(2)
+            ))
         return results
+
+    def transform(pairs, index):
+        return [right_side(left_side([pair], index), index)[0] for pair in pairs]
 
     def times(x, y):
         return x[0] * y[0] - x[1] * y[1], x[0] * y[1] + x[1] * y[0]
@@ -206,24 +211,27 @@
         ]
         if round_index > 0:
             ring.wait_recv()
+            ring.wait_send()
         else:
-            for load in loads[1:4]:
-                load.wait()
+            loads[1].wait()
+            loads[3].wait()
         probe = (probe_src[0], probe_src[1])
         probe_power = total_of(probe[0] ** 2 + probe[1] ** 2) / (window * window) + power_epsilon
-        arrivals = transform([times(probe, objects[0][j]) for j in range(slots)], 4, 4, 1)
+        arrivals = transform([times(probe, objects[0][j]) for j in range(slots)], 0)
         if round_index == 0:
-            for load in loads[4:]:
-                load.wait()
+            loads[2].wait()
             unfold_amps()
-        far = transform([times(arrivals[j], objects[1][j]) for j in range(slots)], 0, 0, 1)
+            loads[4].wait()
+        far = transform([times(arrivals[j], objects[1][j]) for j in range(slots)], 1)
         changes = []
         for j in range(slots):
             weight = jnp.where(counts_ref[0] > j, 1.0, 0.0)
             modulus = jnp.sqrt(over_modes(far[j][0] ** 2 + far[j][1] ** 2))
             factor = widened((amps_ref[j] / jnp.maximum(modulus, modulus_floor) - 1.0) * weight)
             changes.append((far[j][0] * factor, far[j][1] * factor))
-        exits = transform(changes, 2, 0, -1)
+        if round_index == 0:
+            loads[5].wait()
+        exits = transform(changes, 2)
 
         second_gain = object_rate / (probe_power * powers[0] * slots)
         for part in range(2):
@@ -235,7 +243,9 @@
         if last:
             send_rims(1)
 
-        entries = transform([conj_times(objects[1][j], exits[j]) for j in range(slots)], 6, 4, -1)
+        if round_index == 0:
+            loads[6].wait()
+        entries = transform([conj_times(objects[1][j], exits[j]) for j in range(slots)], 3)
         probe_gain = probe_rate / (powers[0] * powers[1] * slots)
         terms = [conj_times(objects[0][j], entries[j]) for j in range(slots)]
         moved = []
@@ -282,8 +292,6 @@
             tile[part, 0] = total
         if last:
             send_rims(0)
-        else:
-            ring.wait_send()
 
     own = shares[b]
     for k in range(1, n_blk):
@@ -354,7 +362,7 @@
     slots = scan_rows.shape[0]
     size = objects.shape[2]
     share = width // n_blk
-    left, right = tables_of(window, width // window)
+    tables = tables_of(window, width // window)
     smem = pl.BlockSpec(memory_space=pltpu.SMEM)
     vmem = pl.BlockSpec(memory_space=pltpu.VMEM)
     dma = pltpu.SemaphoreType.DMA
@@ -364,14 +372,13 @@
             pltpu.VMEM(objects.shape, jnp.float32),
             pltpu.VMEM((2, window, share), jnp.float32),
         ),
-        in_specs=[smem] * 4 + [pl.BlockSpec(memory_space=pltpu.HBM)] * 5,
+        in_specs=[smem] * 4 + [pl.BlockSpec(memory_space=pltpu.HBM)] * 4,
         out_specs=(vmem, vmem),
         scratch_shapes=[
             pltpu.VMEM(objects.shape, jnp.float32),
             pltpu.VMEM(probe_init.shape, jnp.float32),
             pltpu.VMEM(amplitudes.shape, jnp.float32),
-            pltpu.VMEM(left.shape, jnp.bfloat16),
-            pltpu.VMEM(right.shape, jnp.bfloat16),
+            pltpu.VMEM(tables.shape, jnp.bfloat16),
             pltpu.VMEM((slots, window, 128), jnp.float32),
             dma((7,)),
             pltpu.VMEM(objects.shape, jnp.float32),
@@ -394,7 +401,7 @@
     )(
         scan_rows, scan_cols, counts, offsets,
         objects, probe_init, amplitudes,
-        jnp.asarray(left), jnp.asarray(right),
+        jnp.asarray(tables),
     )
 
 

time: 27.3 us -> 25.4 us (0.930)
  Pallas kernels: 24.4 us -> 22.6 us
    pallas_call x1, Pallas kernels: 24.4 us -> 22.6 us  [shards(): pl.pallas_call(functools.partial(kernel, n_strip, n_blk), out_shape=(pltp...]
where the time goes in v2:
time: 25.4 us; the launch traced here: 25.3 us
  Pallas kernels  22.6 us (89%)
  local copies, waits for them, and re-layouts  1.39 us (5%)
  between operations  1.29 us (5%)
    pallas_call x1, Pallas kernels, shards(): pl.pallas_call(functools.partial(kernel, n_strip, n_blk), out_shape=(pltp...  22.6 us
    unnamed x1, local copies, waits for them, and re-layouts  0.71 us
    pallas_call x1, local copies, waits for them, and re-layouts, shards(): pl.pallas_call(functools.partial(kernel, n_strip, n_blk), out_shape=(pltp...  0.69 us

profile of v2, /device:TPU:0, one launch (start us, length us, event | category | flops | bytes accessed | tf_op | source)
XLA Modules:
  0.0 25.3 jit_solution(3524121653773210717)
XLA Ops:
  1.3 22.6 %shard_map.95 = (f32[2,2,128,128]{3,2,1,0:T(8,128)S(1)}, f32[2,64,32]{2,1,0:T(8,128)S(1)}) custom-call(s32[2]{0:T(128)} %rows_ref.1, s32[2]{0:T(128)} %cols_ref.1, s32[1]{0:T(128)S(6)} %copy.13.counts_ref, s32[4]{0:T(128)} %offsets_ref.1, f32[2,2,128,128]{3,2,1,0:T(8,128)} %objects_hbm.1, f32[2,64,256]{2,1,0:T(8,128)} %probe_hbm.1, f32[2,4096]{1,0:T(2,128)} %amps_hbm.1, ...), custom_call_target="tpu_custom_call" | custom-call | tf_op jit(solution)/shard_map/pallas_call | solution.py:369
  23.9 0.7 %copy.12 = f32[2,2,128,128]{3,2,1,0:T(8,128)} copy(f32[2,2,128,128]{3,2,1,0:T(8,128)S(1)} %get-tuple-element.4) | data formatting | bytes 524288
  24.6 0.7 %copy.10 = f32[2,64,32]{1,2,0:T(8,128)} copy(f32[2,64,32]{2,1,0:T(8,128)S(1)} %get-tuple-element.3) | data formatting | bytes 32768 | tf_op jit(solution)/shard_map/pallas_call | solution.py:369

commit v3 on v2

--- a/solution.py
+++ b/solution.py
@@ -11,6 +11,7 @@
 
 ROUNDS = 2
 BORDER = 32
+RING_CHUNKS = 4
 object_rate = 0.3
 probe_rate = 0.5
 modulus_floor = 0.25
@@ -189,11 +190,24 @@
             def _():
                 rim_copy(layer, kind).start()
 
-    ring = pltpu.make_async_remote_copy(
-        src_ref=probe_out, dst_ref=probe_in,
-        send_sem=ring_sems.at[0], recv_sem=ring_sems.at[1],
-        device_id=(s, blk_step(1)), device_id_type=MESH,
-    )
+    chunk = window // RING_CHUNKS
+    chunks = [slice(i * chunk, (i + 1) * chunk) for i in range(RING_CHUNKS)]
+
+    def ring_copy(i):
+        rows = pl.ds(i * chunk, chunk)
+        return pltpu.make_async_remote_copy(
+            src_ref=probe_out.at[:, rows, :], dst_ref=probe_in.at[:, rows, :],
+            send_sem=ring_sems.at[0, i], recv_sem=ring_sems.at[1, i],
+            device_id=(s, blk_step(1)), device_id_type=MESH,
+        )
+
+    ring = [ring_copy(i) for i in range(RING_CHUNKS)]
+
+    def cut(pair, rows):
+        return pair[0][rows], pair[1][rows]
+
+    def joined(pieces):
+        return tuple(jnp.concatenate([piece[part] for piece in pieces], axis=0) for part in range(2))
 
     for round_index in range(ROUNDS):
         last = round_index == ROUNDS - 1
@@ -210,14 +224,21 @@
             for layer in range(2)
         ]
         if round_index > 0:
-            ring.wait_recv()
-            ring.wait_send()
+            middles = []
+            for i in range(RING_CHUNKS):
+                ring[i].wait_recv()
+                piece = (probe_in[0, pl.ds(i * chunk, chunk)], probe_in[1, pl.ds(i * chunk, chunk)])
+                middles.append(right_side([times(piece, cut(objects[0][j], chunks[i])) for j in range(slots)], 0))
+            arrivals = left_side([joined([piece[j] for piece in middles]) for j in range(slots)], 0)
+            for copy in ring:
+                copy.wait_send()
         else:
             loads[1].wait()
             loads[3].wait()
         probe = (probe_src[0], probe_src[1])
         probe_power = total_of(probe[0] ** 2 + probe[1] ** 2) / (window * window) + power_epsilon
-        arrivals = transform([times(probe, objects[0][j]) for j in range(slots)], 0)
+        if round_index == 0:
+            arrivals = transform([times(probe, objects[0][j]) for j in range(slots)], 0)
         if round_index == 0:
             loads[2].wait()
             unfold_amps()
@@ -240,27 +261,36 @@
                 update = over_modes(conj_times(arrivals[j], exits[j])[part]) * second_gain
                 total = total + placed(2 * j + part, update, j)
             tile[part, 1] = total
-        if last:
-            send_rims(1)
 
         if round_index == 0:
             loads[6].wait()
-        entries = transform([conj_times(objects[1][j], exits[j]) for j in range(slots)], 3)
+        returns = [conj_times(objects[1][j], exits[j]) for j in range(slots)]
         probe_gain = probe_rate / (powers[0] * powers[1] * slots)
-        terms = [conj_times(objects[0][j], entries[j]) for j in range(slots)]
-        moved = []
-        for part in range(2):
-            total = terms[0][part]
-            for j in range(1, slots):
-                total = total + terms[j][part]
-            moved.append(probe[part] + probe_gain * total)
+
+        def moved_probe(pieces, rows):
+            terms = [conj_times(cut(objects[0][j], rows), pieces[j]) for j in range(slots)]
+            moved = []
+            for part in range(2):
+                total = terms[0][part]
+                for j in range(1, slots):
+                    total = total + terms[j][part]
+                moved.append(probe[part][rows] + probe_gain * total)
+            return moved
+
         if not last:
-            for part in range(2):
-                probe_out[part] = moved[part]
             if round_index == 0:
                 pl.semaphore_wait(barrier, len(partners))
-            ring.start()
+            middles = left_side(returns, 3)
+            pieces = []
+            for i in range(RING_CHUNKS):
+                pieces.append(right_side([cut(middle, chunks[i]) for middle in middles], 3))
+                for part, value in enumerate(moved_probe(pieces[i], chunks[i])):
+                    probe_out[part, pl.ds(i * chunk, chunk)] = value
+                ring[i].start()
+            entries = [joined([piece[j] for piece in pieces]) for j in range(slots)]
         else:
+            entries = transform(returns, 3)
+            moved = moved_probe(entries, slice(0, window))
             stacked = jnp.concatenate([moved[0] - probe_ref[0], moved[1] - probe_ref[1]], axis=0)
             group_of = lax.broadcasted_iota(jnp.int32, (share, 128), 1) // share
             for h in range(width // 128):
@@ -283,6 +313,8 @@
                 )
                 share_copies[-1].start()
 
+        if last:
+            send_rims(1)
         first_gain = object_rate / (probe_power * slots)
         for part in range(2):
             total = source[part, 0]
@@ -390,7 +422,7 @@
             pltpu.VMEM((share, 128), jnp.float32),
             pltpu.VMEM((n_strip, share, 128), jnp.float32),
             pltpu.VMEM((4, 2, 2, BORDER, size), jnp.float32),
-            dma((2,)),
+            dma((2, RING_CHUNKS)),
             dma((n_blk,)), dma((n_blk,)),
             dma((n_strip,)), dma((n_strip,)),
             dma((4, 2)), dma((4, 2)),

time: 25.4 us -> 25.1 us (0.988)
  Pallas kernels: 22.6 us -> 22.2 us
    pallas_call x1, Pallas kernels: 22.6 us -> 22.2 us  [shards(): pl.pallas_call(functools.partial(kernel, n_strip, n_blk), out_shape=(pltp...]
where the time goes in v3:
time: 25.1 us; the launch traced here: 24.9 us
  Pallas kernels  22.2 us (88%)
  local copies, waits for them, and re-layouts  1.39 us (6%)
  between operations  1.29 us (5%)
    pallas_call x1, Pallas kernels, shards(): pl.pallas_call(functools.partial(kernel, n_strip, n_blk), out_shape=(pltp...  22.2 us
    unnamed x1, local copies, waits for them, and re-layouts  0.71 us
    pallas_call x1, local copies, waits for them, and re-layouts, shards(): pl.pallas_call(functools.partial(kernel, n_strip, n_blk), out_shape=(pltp...  0.69 us

profile of v3, /device:TPU:0, one launch (start us, length us, event | category | flops | bytes accessed | tf_op | source)
XLA Modules:
  0.0 24.9 jit_solution(1101401477810458181)
XLA Ops:
  1.3 22.2 %shard_map.95 = (f32[2,2,128,128]{3,2,1,0:T(8,128)S(1)}, f32[2,64,32]{2,1,0:T(8,128)S(1)}) custom-call(s32[2]{0:T(128)} %rows_ref.1, s32[2]{0:T(128)} %cols_ref.1, s32[1]{0:T(128)S(6)} %copy.13.counts_ref, s32[4]{0:T(128)} %offsets_ref.1, f32[2,2,128,128]{3,2,1,0:T(8,128)} %objects_hbm.1, f32[2,64,256]{2,1,0:T(8,128)} %probe_hbm.1, f32[2,4096]{1,0:T(2,128)} %amps_hbm.1, ...), custom_call_target="tpu_custom_call" | custom-call | tf_op jit(solution)/shard_map/pallas_call | solution.py:401
  23.5 0.7 %copy.12 = f32[2,2,128,128]{3,2,1,0:T(8,128)} copy(f32[2,2,128,128]{3,2,1,0:T(8,128)S(1)} %get-tuple-element.4) | data formatting | bytes 524288
  24.2 0.7 %copy.10 = f32[2,64,32]{1,2,0:T(8,128)} copy(f32[2,64,32]{2,1,0:T(8,128)S(1)} %get-tuple-element.3) | data formatting | bytes 32768 | tf_op jit(solution)/shard_map/pallas_call | solution.py:401

commit v4 on v3

--- a/solution.py
+++ b/solution.py
@@ -254,14 +254,6 @@
             loads[5].wait()
         exits = transform(changes, 2)
 
-        second_gain = object_rate / (probe_power * powers[0] * slots)
-        for part in range(2):
-            total = source[part, 1]
-            for j in range(slots):
-                update = over_modes(conj_times(arrivals[j], exits[j])[part]) * second_gain
-                total = total + placed(2 * j + part, update, j)
-            tile[part, 1] = total
-
         if round_index == 0:
             loads[6].wait()
         returns = [conj_times(objects[1][j], exits[j]) for j in range(slots)]
@@ -313,6 +305,13 @@
                 )
                 share_copies[-1].start()
 
+        second_gain = object_rate / (probe_power * powers[0] * slots)
+        for part in range(2):
+            total = source[part, 1]
+            for j in range(slots):
+                update = over_modes(conj_times(arrivals[j], exits[j])[part]) * second_gain
+                total = total + placed(2 * j + part, update, j)
+            tile[part, 1] = total
         if last:
             send_rims(1)
         first_gain = object_rate / (probe_power * slots)

time: 25.1 us -> 24.9 us (level)
  no operation moved by 1% of the time
where the time goes in v4:
time: 24.9 us; the launch traced here: 24.7 us
  Pallas kernels  22 us (88%)
  local copies, waits for them, and re-layouts  1.39 us (6%)
  between operations  1.29 us (5%)
    pallas_call x1, Pallas kernels, shards(): pl.pallas_call(functools.partial(kernel, n_strip, n_blk), out_shape=(pltp...  22 us
    unnamed x1, local copies, waits for them, and re-layouts  0.71 us
    pallas_call x1, local copies, waits for them, and re-layouts, shards(): pl.pallas_call(functools.partial(kernel, n_strip, n_blk), out_shape=(pltp...  0.69 us

profile of v4, /device:TPU:0, one launch (start us, length us, event | category | flops | bytes accessed | tf_op | source)
XLA Modules:
  0.0 24.7 jit_solution(11334979289245395988)
XLA Ops:
  1.3 22.0 %shard_map.95 = (f32[2,2,128,128]{3,2,1,0:T(8,128)S(1)}, f32[2,64,32]{2,1,0:T(8,128)S(1)}) custom-call(s32[2]{0:T(128)} %rows_ref.1, s32[2]{0:T(128)} %cols_ref.1, s32[1]{0:T(128)S(6)} %copy.13.counts_ref, s32[4]{0:T(128)} %offsets_ref.1, f32[2,2,128,128]{3,2,1,0:T(8,128)} %objects_hbm.1, f32[2,64,256]{2,1,0:T(8,128)} %probe_hbm.1, f32[2,4096]{1,0:T(2,128)} %amps_hbm.1, ...), custom_call_target="tpu_custom_call" | custom-call | tf_op jit(solution)/shard_map/pallas_call | solution.py:400
  23.3 0.7 %copy.12 = f32[2,2,128,128]{3,2,1,0:T(8,128)} copy(f32[2,2,128,128]{3,2,1,0:T(8,128)S(1)} %get-tuple-element.4) | data formatting | bytes 524288
  24.0 0.7 %copy.10 = f32[2,64,32]{1,2,0:T(8,128)} copy(f32[2,64,32]{2,1,0:T(8,128)S(1)} %get-tuple-element.3) | data formatting | bytes 32768 | tf_op jit(solution)/shard_map/pallas_call | solution.py:400

commit v5 on v4

--- a/solution.py
+++ b/solution.py
@@ -270,14 +270,14 @@
             return moved
 
         if not last:
-            if round_index == 0:
-                pl.semaphore_wait(barrier, len(partners))
             middles = left_side(returns, 3)
             pieces = []
             for i in range(RING_CHUNKS):
                 pieces.append(right_side([cut(middle, chunks[i]) for middle in middles], 3))
                 for part, value in enumerate(moved_probe(pieces[i], chunks[i])):
                     probe_out[part, pl.ds(i * chunk, chunk)] = value
+                if round_index == 0 and i == 0:
+                    pl.semaphore_wait(barrier, len(partners))
                 ring[i].start()
             entries = [joined([piece[j] for piece in pieces]) for j in range(slots)]
         else:

time: 24.9 us -> 24.8 us (level)
  no operation moved by 1% of the time
where the time goes in v5:
time: 24.8 us; the launch traced here: 24.6 us
  Pallas kernels  21.9 us (88%)
  local copies, waits for them, and re-layouts  1.39 us (6%)
  between operations  1.29 us (5%)
    pallas_call x1, Pallas kernels, shards(): pl.pallas_call(functools.partial(kernel, n_strip, n_blk), out_shape=(pltp...  21.9 us
    unnamed x1, local copies, waits for them, and re-layouts  0.71 us
    pallas_call x1, local copies, waits for them, and re-layouts, shards(): pl.pallas_call(functools.partial(kernel, n_strip, n_blk), out_shape=(pltp...  0.69 us

profile of v5, /device:TPU:0, one launch (start us, length us, event | category | flops | bytes accessed | tf_op | source)
XLA Modules:
  0.0 24.6 jit_solution(17069832477343365794)
XLA Ops:
  1.3 21.9 %shard_map.95 = (f32[2,2,128,128]{3,2,1,0:T(8,128)S(1)}, f32[2,64,32]{2,1,0:T(8,128)S(1)}) custom-call(s32[2]{0:T(128)} %rows_ref.1, s32[2]{0:T(128)} %cols_ref.1, s32[1]{0:T(128)S(6)} %copy.13.counts_ref, s32[4]{0:T(128)} %offsets_ref.1, f32[2,2,128,128]{3,2,1,0:T(8,128)} %objects_hbm.1, f32[2,64,256]{2,1,0:T(8,128)} %probe_hbm.1, f32[2,4096]{1,0:T(2,128)} %amps_hbm.1, ...), custom_call_target="tpu_custom_call" | custom-call | tf_op jit(solution)/shard_map/pallas_call | solution.py:400
  23.2 0.7 %copy.12 = f32[2,2,128,128]{3,2,1,0:T(8,128)} copy(f32[2,2,128,128]{3,2,1,0:T(8,128)S(1)} %get-tuple-element.4) | data formatting | bytes 524288
  23.9 0.7 %copy.10 = f32[2,64,32]{1,2,0:T(8,128)} copy(f32[2,64,32]{2,1,0:T(8,128)S(1)} %get-tuple-element.3) | data formatting | bytes 32768 | tf_op jit(solution)/shard_map/pallas_call | solution.py:400
